TPU v7x, 256 devices: a whole 4x4x8 slice. The times are simulated.
256 devices in a mesh: dp: 32 (over y_lo, z, core), rows: 8 (over y_hi, x).
Axes of the slice: x: 4, y: 4 (y_hi: 2, y_lo: 2; y = y_hi * 2 + y_lo), z: 8, core: 2. Of those that a mesh axis runs over, the one named last changes fastest.
Arguments:
- block_input: bfloat16 [64, 48, 48, 768], P('dp', 'rows'), may hold values from -40 to 40
- cotangent: bfloat16 [64, 48, 48, 768], P('dp', 'rows'), may hold values from -6 to 6
- dw_kernel: float32 [49, 768], replicated, may hold values from -0.875 to 0.875
- dw_bias: float32 [768], replicated, may hold values from -3 to 3
- ln_gain: float32 [768], replicated, may hold values from 0.5 to 1.5
- ln_bias: float32 [768], replicated, may hold values from -3 to 3
- w1: bfloat16 [768, 3072], P(None, 'dp'), may hold values from -0.21875 to 0.21875
- b1: bfloat16 [3072], P('dp'), may hold values from -3 to 3
- w2: bfloat16 [3072, 768], P('dp'), may hold values from -0.109375 to 0.109375
- b2: float32 [768], replicated, may hold values from -3 to 3
- gamma: float32 [768], replicated, may hold values from 0.3 to 1.5
Outputs:
- d_input: bfloat16 [64, 48, 48, 768], P('dp', 'rows')
- d_w1: float32 [768, 3072], P(None, 'dp')
- d_b1: float32 [3072], P('dp')
- d_w2: float32 [3072, 768], P('dp')
- param_grads: float32 [54, 768], replicated
All inputs are finite; a program needn't handle non-finite values.
Results may differ from a plain program's by a relative error of at most 0.007.
Values may be sent and summed in bfloat16 or wider, within the bound.
No kernel may reach another device: no remote copies, remote signals or barrier semaphores. Data moves between devices by JAX's collectives and lax.ppermute only.
A program may use at most 128 MiB of HBM per device.

v0:
```python
import math

import jax
import jax.numpy as jnp
from jax import lax
from jax.sharding import PartitionSpec as P

KERNEL = 7


EPSILON = 1e-06
INV_ROOT_TWO = 0.7071067811865476
INV_ROOT_TWO_PI = 0.3989422804014327


def padded_2(cells, sides, width):
    for axis, dim in sides:
        count = lax.axis_size(axis)
        ends = count - 1
        head = lax.slice_in_dim(cells, 0, width, axis=dim)
        tail = lax.slice_in_dim(cells, cells.shape[dim] - width, cells.shape[dim], axis=dim)
        cells = jnp.concatenate(
            [
                lax.ppermute(tail, axis, [(i, (i + 1) % count) for i in range(ends)]),
                cells,
                lax.ppermute(head, axis, [((i + 1) % count, i) for i in range(ends)]),
            ],
            axis=dim,
        )
    return cells


def gelu_value(u):
    return 0.5 * u * (1.0 + lax.erf(u * INV_ROOT_TWO))


def gelu_slope(u):
    return 0.5 * (1.0 + lax.erf(u * INV_ROOT_TWO)) + u * jnp.exp(-0.5 * u * u) * INV_ROOT_TWO_PI


def depthwise(padded, kernel, height, width):
    total = jnp.zeros(padded.shape[:-3] + (height, width, padded.shape[-1]), jnp.float32)
    for row_tap in range(KERNEL):
        for col_tap in range(KERNEL):
            window = padded[..., row_tap : row_tap + height, col_tap : col_tap + width, :].astype(
                jnp.float32
            )
            total = total + window * kernel[row_tap * KERNEL + col_tap]
    return total


def transposed(padded_grad, kernel, height, width):
    reach = KERNEL - 1
    total = jnp.zeros(padded_grad.shape[:-3] + (height, width, padded_grad.shape[-1]), jnp.float32)
    for row_tap in range(KERNEL):
        for col_tap in range(KERNEL):
            window = padded_grad[
                ...,
                reach - row_tap : reach - row_tap + height,
                reach - col_tap : reach - col_tap + width,
                :,
            ].astype(jnp.float32)
            total = total + window * kernel[row_tap * KERNEL + col_tap]
    return total


def tap_sums(padded, grad_conv, height, width):
    axes_all = tuple(range(grad_conv.ndim - 1))
    result_rows = []
    for row_tap in range(KERNEL):
        for col_tap in range(KERNEL):
            window = padded[..., row_tap : row_tap + height, col_tap : col_tap + width, :].astype(
                jnp.float32
            )
            result_rows.append(jnp.sum(window * grad_conv, axis=axes_all))
    return jnp.stack(result_rows)


def normalize(conv):
    center = conv - jnp.mean(conv, axis=-1, keepdims=True)
    spread = jnp.mean(center * center, axis=-1, keepdims=True)
    rstd = lax.rsqrt(spread + EPSILON)
    return (center * rstd, rstd)


def norm_backward(grad_normed, norm, rstd, ln_gain):
    weighted = grad_normed * ln_gain
    return rstd * (
        weighted
        - jnp.mean(weighted, axis=-1, keepdims=True)
        - norm * jnp.mean(weighted * norm, axis=-1, keepdims=True)
    )


def shards(block_input, cotangent, dw_kernel, dw_bias, ln_gain, ln_bias, w1, b1, w2, b2, gamma):
    images, rows_here, cols, chans = block_input.shape
    margin = KERNEL // 2
    padded = padded_2(block_input, (("rows", 1),), margin)
    padded = jnp.pad(padded, ((0, 0), (0, 0), (margin, margin), (0, 0)))
    full_w1, full_w2, full_b1 = (
        lax.all_gather(w1, "dp", axis=1, tiled=True),
        lax.all_gather(w2, "dp", axis=0, tiled=True),
        lax.all_gather(b1, "dp", axis=0, tiled=True),
    )
    conv = depthwise(padded, dw_kernel, rows_here, cols) + dw_bias
    norm, rstd = normalize(conv)
    normed = (norm * ln_gain + ln_bias).astype(jnp.bfloat16).reshape(-1, chans)
    preact = jnp.dot(normed, full_w1, preferred_element_type=jnp.float32) + full_b1.astype(
        jnp.float32
    )
    hidden = gelu_value(preact).astype(jnp.bfloat16)
    flat_cot = cotangent.reshape(-1, chans).astype(jnp.float32)
    scaled = (flat_cot * gamma).astype(jnp.bfloat16)
    grad_hidden = lax.dot_general(
        scaled, full_w2, (((1,), (1,)), ((), ())), preferred_element_type=jnp.float32
    )
    grad_preact = (grad_hidden * gelu_slope(preact)).astype(jnp.bfloat16)
    grad_normed = lax.dot_general(
        grad_preact, full_w1, (((1,), (1,)), ((), ())), preferred_element_type=jnp.float32
    ).reshape(conv.shape)
    grad_conv = norm_backward(grad_normed, norm, rstd, ln_gain).astype(jnp.bfloat16)
    grad_padded = padded_2(grad_conv, (("rows", 1),), margin)
    grad_padded = jnp.pad(grad_padded, ((0, 0), (0, 0), (margin, margin), (0, 0)))
    d_input = (
        cotangent.astype(jnp.float32) + transposed(grad_padded, dw_kernel, rows_here, cols)
    ).astype(jnp.bfloat16)
    moment = lax.dot_general(
        hidden, scaled, (((0,), (0,)), ((), ())), preferred_element_type=jnp.float32
    )
    term_w1 = lax.dot_general(
        normed, grad_preact, (((0,), (0,)), ((), ())), preferred_element_type=jnp.float32
    )
    term_b1 = jnp.sum(grad_preact.astype(jnp.float32), axis=0)
    grad_wide = grad_conv.astype(jnp.float32)
    cot_sums = jnp.sum(flat_cot, axis=0)
    local_small = jnp.concatenate(
        [
            tap_sums(padded, grad_wide, rows_here, cols),
            jnp.sum(grad_wide, axis=(0, 1, 2))[None],
            jnp.sum(grad_normed * norm, axis=(0, 1, 2))[None],
            jnp.sum(grad_normed, axis=(0, 1, 2))[None],
            (gamma * cot_sums)[None],
            (jnp.sum(full_w2.astype(jnp.float32) * moment, axis=0) / gamma + b2 * cot_sums)[None],
        ],
        axis=0,
    )
    share_w1, share_w2, share_b1 = (
        lax.psum_scatter(term_w1, "dp", scatter_dimension=1, tiled=True),
        lax.psum_scatter(moment, "dp", scatter_dimension=0, tiled=True),
        lax.psum_scatter(term_b1, "dp", scatter_dimension=0, tiled=True),
    )
    total_w1, total_w2, total_b1 = lax.psum((share_w1, share_w2, share_b1), "rows")
    param_total = lax.psum(local_small, ("dp", "rows"))
    pixel_count = images * rows_here * cols * lax.axis_size("dp") * lax.axis_size("rows")
    factor = 1.0 / math.sqrt(pixel_count)
    return (d_input, total_w1 * factor, total_b1 * factor, total_w2 * factor, param_total * factor)


def solution(mesh):
    placed = (
        P("dp", "rows", None, None),
        P("dp", "rows", None, None),
        P(),
        P(),
        P(),
        P(),
        P(None, "dp"),
        P("dp"),
        P("dp", None),
        P(),
        P(),
    )
    return jax.shard_map(
        shards,
        mesh=mesh,
        in_specs=placed,
        out_specs=(P("dp", "rows", None, None), P(None, "dp"), P("dp"), P("dp", None), P()),
        check_vma=False,
    )
```

profile of v0, /device:TPU:2, one launch (start us, length us, event | category | flops | bytes accessed | tf_op | source)
XLA Modules:
  0.0 794.6 jit_solution(3902654500864067727)
XLA Ops:
  10.0 3.4 collective-permute-start
  13.4 2.5 collective-permute-start.1
  19.5 60.6 %all-reduce.2 = bf16[3072]{0:T(1024)(128)(2,1)S(1)} all-reduce(bf16[3072]{0:T(1024)(128)(2,1)S(1)} %dynamic-update-slice), channel_id=1, replica_groups=mesh['dp'=32,'rows'=8] {'dp'}, use_global_device_ids=true, to_apply=%add.2 | all-reduce | flops 3072 | bytes 12288
  83.2 2.4 fusion.14
  85.7 13.5 %fusion.145 = (f32[2,6,48]{2,1,0:T(8,128)S(1)}, f32[2,6,48,768]{3,2,1,0:T(8,128)S(1)}) fusion(f32[768]{0:T(1024)S(1)} %copy-done.29, f32[768]{0:T(1024)S(1)} %copy-done.22, bf16[2,12,54,768]{3,2,1,0:T(8,128)(2,1)S(1)} %fusion.14, f32[768]{0:T(1024)S(1)} %copy-done.23, f32[768]{0:T(1024)S(1)} %get-tuple-element.67, f32[768]{0:T(1024)S(1)} %get-tuple-element.68, ...), kind=kLoop, calls=%fused_computation.336 | loop fusion | flops 65469888 | bytes 45277440 | tf_op jit(solution)/shard_map/reduce_sum | solution.py:80
  101.7 8.6 %fusion.150 = f32[576,3072]{1,0:T(8,128)} fusion(bf16[576,768]{1,0:T(8,128)(2,1)} %bitcast.19, bf16[768,3072]{0,1:T(8,128)(2,1)} %all-gather.5.cloned.1.call-done), kind=kOutput, calls=%fused_computation.340 | convolution fusion | flops 2717908992 | bytes 12681216 | tf_op jit(solution)/shard_map/dot_general | solution.py:108
  110.3 43.9 %all-gather.3.cloned.1.call-done = bf16[3072,768]{1,0:T(8,128)(2,1)} async-done(((bf16[96,768]{1,0:T(8,128)(2,1)}), bf16[3072,768]{1,0:T(8,128)(2,1)}) %all-gather.3.cloned.1.call-update) | async-done | bytes 4718608 | tf_op jit(solution)/shard_map/all_gather | solution.py:102
  154.2 8.5 %convert_reduce_fusion.1 = (f32[3072]{0:T(1024)}, bf16[576,3072]{1,0:T(8,128)(2,1)S(1)}) fusion(f32[576,3072]{1,0:T(8,128)} %fusion.150, f32[3072]{0:T(1024)S(1)} %copy-done.28, bf16[576,768]{1,0:T(8,128)(2,1)S(1)} %copy-done.10, bf16[3072,768]{1,0:T(8,128)(2,1)} %all-gather.3.cloned.1.call-done), kind=kOutput, calls=%fused_computation.60 | convolution fusion | flops 2740909056 | bytes 16244736 | tf_op jit(solution)/shard_map/dot_general | solution.py:114
  162.7 3.0 fusion.144
  167.2 6.5 fusion.135
  173.7 3.1 fusion.134
  176.9 4.7 fusion.136
  182.1 6.7 multiply_reduce_fusion
  189.0 4.5 concatenate.35
  193.6 9.0 %fusion.151 = f32[768,3072]{0,1:T(8,128)} fusion(bf16[576,768]{1,0:T(8,128)(2,1)S(1)} %bitcast.20, bf16[576,3072]{1,0:T(8,128)(2,1)} %copy-done.35), kind=kOutput, calls=%fused_computation.341 | convolution fusion | flops 2717908992 | bytes 13860864 | tf_op jit(solution)/shard_map/dot_general | solution.py:130
  204.1 3.4 collective-permute-start.2
  207.5 2.5 collective-permute-start.3
  210.0 105.2 %all-reduce.3 = f32[3072]{0:T(1024)S(1)} all-reduce(f32[3072]{0:T(1024)S(1)} %copy-done.27), channel_id=3, replica_groups=mesh['dp'=32,'rows'=8] {'dp'}, use_global_device_ids=true, to_apply=%region_7.8.clone | all-reduce | flops 3072 | bytes 24576
  315.3 19.8 %psum.29 = f32[96]{0:T(128)S(1)} all-reduce(f32[96]{0:T(128)S(1)} %dynamic-slice.2), channel_id=1, replica_groups=mesh['dp'=32,'rows'=8] {'rows'}, use_global_device_ids=true, to_apply=%region_8.9 | all-reduce | flops 96 | bytes 768 | tf_op jit(solution)/shard_map/psum | solution.py:152
  335.6 101.3 %all-reduce.8.cloned.1.call-done = f32[54,768]{1,0:T(8,128)} async-done(((f32[54,768]{1,0:T(8,128)}), f32[54,768]{1,0:T(8,128)}) %all-reduce.8.cloned.1.call-update) | async-done | bytes 165904 | tf_op jit(solution)/shard_map/psum | solution.py:153
  440.4 128.5 %reduce-scatter.3.cloned.1.call-done = f32[768,96]{0,1:T(8,128)} async-done(((f32[768,3072]{0,1:T(8,128)}), f32[768,96]{0,1:T(8,128)}) %reduce-scatter.3.cloned.1.call-update) | async-done | bytes 294928 | tf_op jit(solution)/shard_map/reduce_scatter | solution.py:148
  568.9 129.5 %reduce-scatter.5.cloned.1.call-done = f32[96,768]{1,0:T(8,128)} async-done(((f32[3072,768]{1,0:T(8,128)}), f32[96,768]{1,0:T(8,128)}) %reduce-scatter.5.cloned.1.call-update) | async-done | bytes 294928 | tf_op jit(solution)/shard_map/reduce_scatter | solution.py:149
  698.4 14.9 %add_convert_fusion = bf16[2,6,48,768]{3,2,1,0:T(8,128)(2,1)} fusion(bf16[2,6,48,768]{3,2,1,0:T(8,128)(2,1)S(1)} %get-tuple-element.117, bf16[2,3,48,768]{3,2,1,0:T(8,128)(2,1)S(1)} %collective-permute-done.2, bf16[2,3,48,768]{3,2,1,0:T(8,128)(2,1)} %collective-permute-done.3, bf16[2,12,54,768]{3,2,1,0:T(8,128)(2,1)S(1)} %select_maximum_fusion, ...), kind=kLoop, calls=%fused_computation.249 | loop fusion | flops 68567040 | bytes 40848384 | tf_op jit(solution)/shard_map/convert_element_type | solution.py:126
  713.3 71.1 %all-reduce.10.cloned.1.call-done = (f32[768,96]{0,1:T(8,128)}, f32[96,768]{1,0:T(8,128)}) async-done(((f32[768,96]{0,1:T(8,128)}, f32[96,768]{1,0:T(8,128)}), (f32[768,96]{0,1:T(8,128)}, f32[96,768]{1,0:T(8,128)})) %all-reduce.10.cloned.1.call-update) | async-done | bytes 589840 | tf_op jit(solution)/shard_map/psum | solution.py:152
  (182 shorter events, 21.1 us)
Async XLA Ops:
  7.2 9.7 %copy-start.32 = (u32[256]{0:T(256)S(1)}, u32[256]{0:T(256)}, u32[]{:S(2)}) copy-start(u32[256]{0:T(256)} %constant.36) | copy-start | bytes 3076
  7.2 8.7 %copy-start.13 = (f32[49,768]{1,0:T(8,128)S(1)}, f32[49,768]{1,0:T(8,128)}, u32[]{:S(2)}) copy-start(f32[49,768]{1,0:T(8,128)} %param.13) | copy-start | bytes 451588
  7.2 10.3 %copy-start.8 = (bf16[2,6,48,768]{3,2,1,0:T(8,128)(2,1)S(1)}, bf16[2,6,48,768]{3,2,1,0:T(8,128)(2,1)}, u32[]{:S(2)}) copy-start(bf16[2,6,48,768]{3,2,1,0:T(8,128)(2,1)} %param.12) | copy-start | bytes 2654212
  7.2 10.3 %copy-start.24 = (f32[768]{0:T(1024)S(1)}, f32[768]{0:T(1024)}, u32[]{:S(2)}) copy-start(f32[768]{0:T(1024)} %param.21) | copy-start | bytes 9220
  7.2 94.5 %all-gather.5.cloned.1.call-start = ((), (), s32[]{:S(2)}) async-start(), calls=%async_computation.3 | async-start | bytes 4866048 | tf_op jit(solution)/shard_map/all_gather | solution.py:101
  7.9 146.2 %all-gather.3.cloned.1.call-start = ((), (), s32[]{:S(2)}) async-start(), calls=%async_computation.2 | async-start | bytes 4866048 | tf_op jit(solution)/shard_map/all_gather | solution.py:102
  8.7 10.6 %copy-start.34 = (bf16[96]{0:T(256)(128)(2,1)S(1)}, bf16[96]{0:T(256)(128)(2,1)}, u32[]{:S(2)}) copy-start(bf16[96]{0:T(256)(128)(2,1)} %param.18) | copy-start | bytes 580
  8.7 428.2 %all-reduce.8.cloned.1.call-start = ((), (), s32[]{:S(2)}) async-start(), calls=%async_computation.6 | async-start | bytes 344064 | tf_op jit(solution)/shard_map/psum | solution.py:153
  10.0 71.5 %collective-permute-start = (bf16[2,3,48,768]{3,2,1,0:T(8,128)(2,1)S(1)}, bf16[2,3,48,768]{3,2,1,0:T(8,128)(2,1)S(1)}, u32[]{:S(2)}, u32[]{:S(2)}) collective-permute-start(bf16[2,3,48,768]{3,2,1,0:T(8,128)(2,1)S(1)} %get-tuple-element.124), channel_id=1, source_target_pairs={{0,1},{1,2},{2,3},{3,4},{4,5},{5,6},{6,7},{8,9},{9,10},{10,11},{11... | collective-permute-start | bytes 1327112 | tf_op jit(solution)/shard_map/ppermute | solution.py:24
  13.4 68.3 %collective-permute-start.1 = (bf16[2,3,48,768]{3,2,1,0:T(8,128)(2,1)S(1)}, bf16[2,3,48,768]{3,2,1,0:T(8,128)(2,1)}, u32[]{:S(2)}, u32[]{:S(2)}) collective-permute-start(bf16[2,3,48,768]{3,2,1,0:T(8,128)(2,1)S(1)} %get-tuple-element.125), channel_id=1, source_target_pairs={{1,0},{2,1},{3,2},{4,3},{5,4},{6,5},{7,6},{9,8},{10,9},{11,10},{12... | collective-permute-start | bytes 1327112 | tf_op jit(solution)/shard_map/ppermute | solution.py:26
  17.5 64.1 %copy-start.6 = (bf16[2,6,48,768]{3,2,1,0:T(8,128)(2,1)S(1)}, bf16[2,6,48,768]{3,2,1,0:T(8,128)(2,1)}, u32[]{:S(2)}) copy-start(bf16[2,6,48,768]{3,2,1,0:T(8,128)(2,1)} %param.11) | copy-start | bytes 2654212
  101.7 52.5 %copy-start.10 = (bf16[576,768]{1,0:T(8,128)(2,1)S(1)}, bf16[576,768]{1,0:T(8,128)(2,1)}, u32[]{:S(2)}) copy-start(bf16[576,768]{1,0:T(8,128)(2,1)} %fusion.137) | copy-start | bytes 2654212
  101.7 52.5 %copy-start.28 = (f32[3072]{0:T(1024)S(1)}, f32[3072]{0:T(1024)}, u32[]{:S(2)}) copy-start(f32[3072]{0:T(1024)} %convert_element_type.438) | copy-start | bytes 36868
  154.2 8.5 %copy-start.33 = (bf16[768,3072]{0,1:T(8,128)(2,1)S(1)}, bf16[768,3072]{0,1:T(8,128)(2,1)}, u32[]{:S(2)}) copy-start(bf16[768,3072]{0,1:T(8,128)(2,1)} %all-gather.5.cloned.1.call-done) | copy-start | bytes 14155780
  173.7 8.2 %slice-start = ((s8[4718592]{0:T(1024)(128)(4,1)}), s8[4194304]{0:T(1024)(128)(4,1)S(1)}, s32[]{:S(2)}) async-start(s8[4718592]{0:T(1024)(128)(4,1)} %bitcast.21), calls=%async_computation.8 | async-start | bytes 8388608
  173.7 8.2 %slice-start.2 = ((s8[7077888]{0:T(1024)(128)(4,1)}), s8[4194304]{0:T(1024)(128)(4,1)S(1)}, s32[]{:S(2)}) async-start(s8[7077888]{0:T(1024)(128)(4,1)} %bitcast.23), calls=%async_computation.10 | async-start | bytes 8388608
  182.0 6.7 copy-start.25
  182.0 6.7 copy-start.26
  182.1 11.6 %copy-start.12 = (bf16[2,6,48,768]{3,2,1,0:T(8,128)(2,1)S(1)}, bf16[2,6,48,768]{3,2,1,0:T(8,128)(2,1)}, u32[]{:S(2)}) copy-start(bf16[2,6,48,768]{3,2,1,0:T(8,128)(2,1)} %add_convert_fusion.1) | copy-start | bytes 2654212
  193.6 375.3 %reduce-scatter.3.cloned.1.call-start = ((), (), s32[]{:S(2)}) async-start(), calls=%async_computation.4 | async-start | bytes 9732096 | tf_op jit(solution)/shard_map/reduce_scatter | solution.py:148
  202.7 495.7 %reduce-scatter.5.cloned.1.call-start = ((), (), s32[]{:S(2)}) async-start(), calls=%async_computation.5 | async-start | bytes 9732096 | tf_op jit(solution)/shard_map/reduce_scatter | solution.py:149
  203.3 581.0 %all-reduce.10.cloned.1.call-start = ((), (), s32[]{:S(2)}) async-start(), calls=%async_computation.7 | async-start | bytes 1179648 | tf_op jit(solution)/shard_map/psum | solution.py:152
  204.1 234.4 %collective-permute-start.2 = (bf16[2,3,48,768]{3,2,1,0:T(8,128)(2,1)S(1)}, bf16[2,3,48,768]{3,2,1,0:T(8,128)(2,1)S(1)}, u32[]{:S(2)}, u32[]{:S(2)}) collective-permute-start(bf16[2,3,48,768]{3,2,1,0:T(8,128)(2,1)S(1)} %get-tuple-element.121), channel_id=1, source_target_pairs={{0,1},{1,2},{2,3},{3,4},{4,5},{5,6},{6,7},{8,9},{9,10},{10,11},{11... | collective-permute-start | bytes 1327112 | tf_op jit(solution)/shard_map/ppermute | solution.py:24
  207.5 231.1 %collective-permute-start.3 = (bf16[2,3,48,768]{3,2,1,0:T(8,128)(2,1)S(1)}, bf16[2,3,48,768]{3,2,1,0:T(8,128)(2,1)}, u32[]{:S(2)}, u32[]{:S(2)}) collective-permute-start(bf16[2,3,48,768]{3,2,1,0:T(8,128)(2,1)S(1)} %get-tuple-element.120), channel_id=1, source_target_pairs={{1,0},{2,1},{3,2},{4,3},{5,4},{6,5},{7,6},{9,8},{10,9},{11,10},{12... | collective-permute-start | bytes 1327112 | tf_op jit(solution)/shard_map/ppermute | solution.py:26
  (26 other events, 90.6 us)
Sparse Core Ops, SparseCore 0:
  9.9 71.1 all-gather.4
  83.0 71.1 all-gather.2
  193.7 243.1 all-reduce.7
  439.3 129.5 reduce-scatter.2
  571.3 127.0 reduce-scatter.4
  700.9 83.3 all-reduce.9
where the time goes:
time: 798 us; the launch traced here: 795 us
  waiting for transfers between devices  476 us (60%)
  blocking collectives  186 us (23%)
  other arithmetic  57.3 us (7%)
  matrix products  35.8 us (4%)
  between operations  16.5 us (2%)
  starting transfers between devices  12 us (2%)
  local copies, waits for them, and re-layouts  11.2 us (1%)
    unnamed x2, blocking collectives  166 us
    reduce_scatter x1, waiting for transfers between devices, shards(): lax.psum_scatter(moment, 'dp', scatter_dimension=0, tiled=True)  129 us
    reduce_scatter x1, waiting for transfers between devices, shards(): lax.psum_scatter(term_w1, 'dp', scatter_dimension=1, tiled=True)  128 us
    psum x1, waiting for transfers between devices, shards(): param_total = lax.psum(local_small, ('dp', 'rows'))  101 us
    psum x1, waiting for transfers between devices, shards(): lax.psum((share_w1, share_w2, share_b1), 'rows')  71.1 us
    all_gather x1, waiting for transfers between devices, shards(): lax.all_gather(w2, 'dp', axis=0, tiled=True)  43.9 us
    psum x1, blocking collectives, shards(): lax.psum((share_w1, share_w2, share_b1), 'rows')  19.8 us
  transfers between devices with their start and end apart: 10, of which 5 were waited for; matrix products, arithmetic and copies ran while one was open for 8% of the time, Pallas kernels for 0%

commit v1 on v0

v1 whole, which is shorter than its diff:
```python
import math

import jax
import jax.numpy as jnp
import numpy as np
from jax import lax
from jax.sharding import Mesh, PartitionSpec as P

KERNEL = 7
MARGIN = 3
EPSILON = 1e-06
INV_ROOT_TWO = 0.7071067811865476
INV_ROOT_TWO_PI = 0.3989422804014327

AXES = ("y_lo", "z", "core", "y_hi", "x")
SIZES = (2, 8, 2, 2, 4)
DP = ("y_lo", "z", "core")
ROWS = ("y_hi", "x")
PAIRS = ("y_lo", "z")


def halo(cells):
    down = [(i, i + 1) for i in range(7)]
    up = [(i + 1, i) for i in range(7)]
    above = lax.ppermute(cells[:, -MARGIN:], ROWS, down)
    below = lax.ppermute(cells[:, :MARGIN], ROWS, up)
    return jnp.concatenate([above, cells, below], axis=1)


def swap(cells):
    return lax.ppermute(cells, "core", [(0, 1), (1, 0)])


def spread_sum(part, axes):
    count = lax.axis_size(axes)
    pieces = part.reshape((count, part.shape[0] // count) + part.shape[1:])
    pieces = lax.all_to_all(pieces, axes, 0, 0)
    return jnp.sum(pieces.astype(jnp.float32), axis=0)


def gather(part, axes):
    count = lax.axis_size(axes)
    return lax.all_to_all(jnp.broadcast_to(part[None], (count,) + part.shape), axes, 0, 0)


def total(small):
    size = small.size
    flat = jnp.pad(small.reshape(-1), (0, -size % (16 * 1024))).reshape(16, -1, 128)
    part = spread_sum(flat, ("core",) + ROWS)
    part = jnp.sum(gather(part, PAIRS), axis=0)
    return gather(part, ("core",) + ROWS).reshape(-1)[:size].reshape(small.shape)


def pad_columns(cells):
    return jnp.pad(cells, ((0, 0), (0, 0), (MARGIN, MARGIN), (0, 0)))


def depthwise(padded, kernel, height, width):
    total = jnp.zeros(padded.shape[:-3] + (height, width, padded.shape[-1]), jnp.float32)
    for row_tap in range(KERNEL):
        for col_tap in range(KERNEL):
            window = padded[:, row_tap : row_tap + height, col_tap : col_tap + width]
            total = total + window.astype(jnp.float32) * kernel[row_tap * KERNEL + col_tap]
    return total


def tap_sums(padded, grad_conv, height, width):
    rows = []
    for row_tap in range(KERNEL):
        for col_tap in range(KERNEL):
            window = padded[:, row_tap : row_tap + height, col_tap : col_tap + width]
            rows.append(jnp.sum(window.astype(jnp.float32) * grad_conv, axis=(0, 1, 2)))
    return jnp.stack(rows)


def shards(block_input, cotangent, dw_kernel, dw_bias, ln_gain, ln_bias, w1, b1, w2, b2, gamma):
    images, rows_here, cols, chans = block_input.shape
    shard = w1.shape[1]
    pixels = images * rows_here * cols
    flat_cot = cotangent.reshape(pixels, chans).astype(jnp.float32)
    scaled = (flat_cot * gamma).astype(jnp.bfloat16)
    packed = jnp.concatenate(
        [w1.T, w2, jnp.broadcast_to(b1[:, None], (shard, 128))], axis=1
    )
    weights = lax.all_gather(packed, PAIRS, axis=0, tiled=True)
    w1_t, w2_h = weights[:, :chans], weights[:, chans : 2 * chans]
    b1_h = weights[:, 2 * chans].astype(jnp.float32)

    padded = pad_columns(halo(block_input))
    scaled2 = jnp.concatenate([scaled, swap(scaled)], axis=0)
    conv = depthwise(padded, dw_kernel, rows_here, cols) + dw_bias
    center = conv - jnp.mean(conv, axis=-1, keepdims=True)
    spread = jnp.mean(center * center, axis=-1, keepdims=True)
    rstd = lax.rsqrt(spread + EPSILON).reshape(pixels, 1)
    norm = center.reshape(pixels, chans) * rstd
    normed = (norm * ln_gain + ln_bias).astype(jnp.bfloat16)
    normed2 = jnp.concatenate([normed, swap(normed)], axis=0)

    nt = (((1,), (1,)), ((), ()))
    nn = (((1,), (0,)), ((), ()))
    tn = (((0,), (0,)), ((), ()))
    preact = lax.dot_general(normed2, w1_t, nt, preferred_element_type=jnp.float32) + b1_h
    grad_hidden = lax.dot_general(scaled2, w2_h, nt, preferred_element_type=jnp.float32)
    cdf = 0.5 * (1.0 + lax.erf(preact * INV_ROOT_TWO))
    hidden = (preact * cdf).astype(jnp.bfloat16)
    slope = cdf + preact * jnp.exp(-0.5 * preact * preact) * INV_ROOT_TWO_PI
    grad_preact = (grad_hidden * slope).astype(jnp.bfloat16)

    grad_normed2 = lax.dot_general(grad_preact, w1_t, nn, preferred_element_type=jnp.float32)
    grad_normed = grad_normed2[:pixels] + swap(grad_normed2[pixels:].astype(jnp.bfloat16)).astype(
        jnp.float32
    )
    moment = lax.dot_general(hidden, scaled2, tn, preferred_element_type=jnp.float32)
    term_w1 = lax.dot_general(grad_preact, normed2, tn, preferred_element_type=jnp.float32)
    terms = jnp.concatenate([term_w1, moment], axis=1).astype(jnp.bfloat16)
    share = lax.psum_scatter(terms, PAIRS, scatter_dimension=0, tiled=True)
    share = gather(spread_sum(share, ROWS).astype(jnp.bfloat16), ROWS)
    share = share.reshape(shard, 2 * chans).astype(jnp.float32)

    weighted = grad_normed * ln_gain
    grad_conv = (
        rstd
        * (
            weighted
            - jnp.mean(weighted, axis=-1, keepdims=True)
            - norm * jnp.mean(weighted * norm, axis=-1, keepdims=True)
        )
    ).astype(jnp.bfloat16)
    grad_maps = grad_conv.reshape(block_input.shape)
    grad_padded = pad_columns(halo(grad_maps))
    d_input = (
        cotangent.astype(jnp.float32)
        + depthwise(grad_padded, dw_kernel[::-1], rows_here, cols)
    ).astype(jnp.bfloat16)

    grad_wide = grad_maps.astype(jnp.float32)
    cot_sums = jnp.sum(flat_cot, axis=0)
    core = lax.axis_index("core")
    hid = b1_h.shape[0]
    sums_b1 = jnp.sum(grad_preact.astype(jnp.float32), axis=0)
    pair_b1 = jnp.where(core == jnp.arange(2)[:, None], sums_b1[None], 0.0)
    local_small = jnp.concatenate(
        [
            tap_sums(padded, grad_wide, rows_here, cols),
            jnp.sum(grad_wide, axis=(0, 1, 2))[None],
            jnp.sum(grad_normed * norm, axis=0)[None],
            jnp.sum(grad_normed, axis=0)[None],
            (gamma * cot_sums)[None],
            (jnp.sum(w2_h.astype(jnp.float32) * moment, axis=0) / gamma + b2 * cot_sums)[None],
            pair_b1.reshape(-1, chans),
        ],
        axis=0,
    )
    total_small = total(local_small)
    factor = 1.0 / math.sqrt(pixels * 256)
    param_grads = total_small[:54] * factor
    at = (lax.axis_index("y_lo") * 8 + lax.axis_index("z")) * shard
    d_b1 = lax.dynamic_slice(
        total_small[54:].reshape(2, hid), (core, at), (1, shard)
    ).reshape(shard) * factor
    share = share * factor
    d_w1, d_w2 = share[:, :chans].T, share[:, chans:]
    return (d_input.reshape(block_input.shape), d_w1, d_b1, d_w2, param_grads)


def solution(mesh):
    fine = Mesh(mesh.devices.reshape(SIZES), AXES)
    placed = (
        P(DP, ROWS, None, None),
        P(DP, ROWS, None, None),
        P(),
        P(),
        P(),
        P(),
        P(None, DP),
        P(DP),
        P(DP, None),
        P(),
        P(),
    )
    return jax.shard_map(
        shards,
        mesh=fine,
        in_specs=placed,
        out_specs=(P(DP, ROWS, None, None), P(None, DP), P(DP), P(DP, None), P()),
        check_vma=False,
    )
```

time: 798 us -> 283 us (0.35)
  waiting for transfers between devices: 476 us -> 81.7 us
  blocking collectives: 186 us -> 0 us
  starting transfers between devices: 12 us -> 61.3 us
  local copies, waits for them, and re-layouts: 11.2 us -> 26.7 us
    reduce_scatter x2 -> x1, waiting for transfers between devices: 258 us -> 0.02 us  [shards(): share = lax.psum_scatter(terms, PAIRS, scatter_dimension=0, tiled=True)]
    psum x2 -> x0, waiting for transfers between devices: 172 us -> none  [the longest x1 101 us: shards(): param_total = lax.psum(local_small, ('dp', 'rows'))]
    unnamed x2 -> x0, blocking collectives: 166 us -> none
    all_to_all x0 -> x5, starting transfers between devices: none -> 49 us  [the longest x3 31.7 us: gather(): lax.all_to_all(jnp.broadcast_to(part[None], (count,) + part.shape), axes,...]
    all_to_all x0 -> x5, waiting for transfers between devices: none -> 28.6 us  [the longest x3 22.9 us: gather(): lax.all_to_all(jnp.broadcast_to(part[None], (count,) + part.shape), axes,...]
    psum x1 -> x0, blocking collectives: 19.8 us -> none  [shards(): lax.psum((share_w1, share_w2, share_b1), 'rows')]
    ppermute x4 -> x7, waiting for transfers between devices: 0.01 us -> 11.8 us  [the longest x2 6.56 us: halo(): above = lax.ppermute(cells[:, -MARGIN:], ROWS, down)]
    unnamed x85 -> x118, local copies, waits for them, and re-layouts: 2.6 us -> 11.5 us
  transfers between devices with their start and end apart: 10 -> 14, of which waited for: 5 -> 8; matrix products, arithmetic and copies ran while one was open for 8% -> 28% of each run, Pallas kernels for 0% -> 0%
where the time goes in v1:
time: 283 us; the launch traced here: 280 us
  waiting for transfers between devices  81.7 us (29%)
  other arithmetic  63.6 us (22%)
  starting transfers between devices  61.3 us (22%)
  matrix products  31.5 us (11%)
  local copies, waits for them, and re-layouts  26.7 us (9%)
  between operations  15.6 us (6%)
    all_gather x1, waiting for transfers between devices, shards(): weights = lax.all_gather(packed, PAIRS, axis=0, tiled=True)  41.2 us
    all_to_all x3, starting transfers between devices, gather(): lax.all_to_all(jnp.broadcast_to(part[None], (count,) + part.shape), axes,...  31.7 us
    all_to_all x3, waiting for transfers between devices, gather(): lax.all_to_all(jnp.broadcast_to(part[None], (count,) + part.shape), axes,...  22.9 us
    all_to_all x2, starting transfers between devices, spread_sum(): pieces = lax.all_to_all(pieces, axes, 0, 0)  17.2 us
    convert_element_type x1, other arithmetic, shards(): d_input = (cotangent.astype(jnp.float32) + depthwise(grad_padded, dw_kern...  15.9 us
    reduce_sum x1, other arithmetic, shards(): center = conv - jnp.mean(conv, axis=-1, keepdims=True)  13.9 us
    reduce_sum x3, other arithmetic, tap_sums(): rows.append(jnp.sum(window.astype(jnp.float32) * grad_conv, axis=(0, 1, 2)))  12 us
    unnamed x118, local copies, waits for them, and re-layouts  11.5 us
  transfers between devices with their start and end apart: 14, of which 8 were waited for; matrix products, arithmetic and copies ran while one was open for 28% of the time, Pallas kernels for 0%

profile of v1, /device:TPU:2, one launch (start us, length us, event | category | flops | bytes accessed | tf_op | source)
XLA Modules:
  0.0 280.4 jit_solution(15187331303709709663)
XLA Ops:
  11.1 3.4 %collective-permute-start = (bf16[2,3,48,768]{3,2,1,0:T(8,128)(2,1)S(1)}, bf16[2,3,48,768]{3,2,1,0:T(8,128)(2,1)S(1)}, u32[]{:S(2)}, u32[]{:S(2)}) collective-permute-start(bf16[2,3,48,768]{3,2,1,0:T(8,128)(2,1)S(1)} %get-tuple-element.125), channel_id=1, source_target_pairs={{0,1},{1,2},{2,3},{3,4},{4,5},{5,6},{6,7},{8,9},{9,10},{10,11},{11... | collective-permute-start | bytes 1327112 | tf_op jit(solution)/shard_map/ppermute | solution.py:25
  18.3 6.6 %collective-permute-done = bf16[2,3,48,768]{3,2,1,0:T(8,128)(2,1)S(1)} collective-permute-done((bf16[2,3,48,768]{3,2,1,0:T(8,128)(2,1)S(1)}, bf16[2,3,48,768]{3,2,1,0:T(8,128)(2,1)S(1)}, u32[]{:S(2)}, u32[]{:S(2)}) %collective-permute-start) | collective-permute-done | bytes 442400 | tf_op jit(solution)/shard_map/ppermute | solution.py:25
  29.4 13.9 %fusion.149 = (f32[2,6,48]{2,1,0:T(8,128)S(1)}, f32[2,6,48,768]{3,2,1,0:T(8,128)S(1)}) fusion(f32[768]{0:T(1024)S(1)} %copy-done.51, f32[768]{0:T(1024)S(1)} %get-tuple-element.111, bf16[2,12,54,768]{3,2,1,0:T(8,128)(2,1)S(1)} %fusion.15, f32[768]{0:T(1024)S(1)} %get-tuple-element.112, f32[768]{0:T(1024)S(1)} %get-tuple-element.65, ...), kind=kLoop, calls=%fused_computation.353 | loop fusion | flops 65469888 | bytes 45277440 | tf_op jit(solution)/shard_map/reduce_sum | solution.py:92
  44.9 3.4 %add_convert_fusion.1 = (bf16[576,768]{1,0:T(8,128)(2,1)}, f32[576,768]{1,0:T(8,128)}) fusion(f32[768]{0:T(1024)S(1)} %copy-done.52, f32[768]{0:T(1024)S(1)} %copy-done.12, f32[576]{0:T(1024)S(1)} %rsqrt.13, f32[2,6,48,768]{3,2,1,0:T(8,128)} %get-tuple-element.118), kind=kLoop, calls=%fused_computation.262 | loop fusion | flops 1769472 | bytes 4432128 | tf_op jit(solution)/shard_map/convert_element_type | solution.py:96
  49.8 41.2 %all-gather.2.cloned.1.call-done = bf16[1536,1664]{1,0:T(8,128)(2,1)} async-done(((bf16[96,1664]{1,0:T(8,128)(2,1)}), bf16[1536,1664]{1,0:T(8,128)(2,1)}) %all-gather.2.cloned.1.call-update) | async-done | bytes 5111824 | tf_op jit(solution)/shard_map/all_gather | solution.py:85
  92.4 5.2 %convolution_add_fusion = f32[1152,1536]{1,0:T(8,128)S(1)} fusion(f32[1536]{0:T(1024)S(1)} %convert_reduce_fusion.3, bf16[1536,1664]{1,0:T(8,128)(2,1)} %all-gather.2.cloned.1.call-done, bf16[576,768]{1,0:T(8,128)(2,1)} %collective-permute-done.3, bf16[576,768]{1,0:T(8,128)(2,1)} %get-tuple-element.115), kind=kOutput, calls=%fused_computation.52 | convolution fusion | flops 2723217408 | bytes 11212800 | tf_op jit(solution)/shard_map/dot_general | solution.py:102
  97.7 7.8 %multiply_reduce_fusion = (f32[768]{0:T(1024)S(1)}, bf16[1536,768]{1,0:T(8,128)(2,1)}) fusion(bf16[1536,1664]{1,0:T(8,128)(2,1)S(1)} %bitcast.29, bf16[576,768]{1,0:T(8,128)(2,1)} %collective-permute-done.2, bf16[576,768]{1,0:T(8,128)(2,1)} %fusion.138, f32[1152,1536]{1,0:T(8,128)S(1)} %convolution_add_fusion), kind=kOutput, calls=%fused_computation.64 | convolution fusion | flops 2735013120 | bytes 13569024 | tf_op jit(solution)/shard_map/dot_general | solution.py:113
  105.4 4.3 %copy.21 = bf16[1536,768]{0,1:T(8,128)(2,1)} copy(bf16[1536,768]{1,0:T(8,128)(2,1)} %get-tuple-element.132) | data formatting | bytes 4718592 | tf_op jit(solution)/shard_map/dot_general | solution.py:113
  109.8 7.7 %convert_reduce_fusion = (f32[1536]{0:T(1024)S(1)}, bf16[1152,1536]{1,0:T(8,128)(2,1)S(1)}) fusion(f32[1152,1536]{1,0:T(8,128)} %copy-done.54, bf16[1536,1664]{1,0:T(8,128)(2,1)} %all-gather.2.cloned.1.call-done, bf16[576,768]{1,0:T(8,128)(2,1)} %collective-permute-done.2, bf16[576,768]{1,0:T(8,128)(2,1)} %fusion.138), kind=kOutput, calls=%fused_computation.58 | convolution fusion | flops 2742680064 | bytes 14751744 | tf_op jit(solution)/shard_map/dot_general | solution.py:103
  119.3 5.1 %convolution_convert_fusion = bf16[1536,768]{0,1:T(8,128)(2,1)S(1)} fusion(bf16[1152,1536]{1,0:T(8,128)(2,1)S(1)} %get-tuple-element.134, bf16[576,768]{1,0:T(8,128)(2,1)} %collective-permute-done.3, bf16[576,768]{1,0:T(8,128)(2,1)} %get-tuple-element.115), kind=kOutput, calls=%fused_computation.67 | convolution fusion | flops 2722627584 | bytes 7667712 | tf_op jit(solution)/shard_map/dot_general | solution.py:114
  126.9 6.6 %copy.23 = bf16[1536,1536]{1,0:T(8,128)(2,1)} copy(bf16[1536,1536]{0,1:T(8,128)(2,1)} %pad_maximum_fusion) | data formatting | bytes 9437184
  133.6 5.7 %fusion.7 = f32[1152,768]{1,0:T(8,128)S(1)} fusion(bf16[1152,1536]{1,0:T(8,128)(2,1)} %copy-done.55, bf16[1536,1664]{1,0:T(8,128)(2,1)} %all-gather.2.cloned.1.call-done), kind=kOutput, calls=%fused_computation.117 | convolution fusion | flops 2717908992 | bytes 9437184 | tf_op jit(solution)/shard_map/dot_general | solution.py:109
  153.8 4.6 %fusion.136 = (f32[768]{0:T(1024)S(1)}, f32[768]{0:T(1024)S(1)}, f32[768]{0:T(1024)S(1)}, f32[768]{0:T(1024)S(1)}, f32[768]{0:T(1024)S(1)}, /*index=5*/f32[768]{...) fusion(bf16[2,6,48,768]{3,2,1,0:T(8,128)(2,1)S(1)} %bitcast.22,, ...), kind=kLoop, calls=%fused_computation.248 | loop fusion | flops 24316416 | bytes 16865280 | tf_op jit(solution)/shard_map/reduce_sum | solution.py:72
  158.4 4.7 %fusion.137 = (f32[768]{0:T(1024)S(1)}, f32[768]{0:T(1024)S(1)}, f32[768]{0:T(1024)S(1)}, f32[768]{0:T(1024)S(1)}, f32[768]{0:T(1024)S(1)}, /*index=5*/f32[768]{...) fusion(bf16[2,6,48,768]{3,2,1,0:T(8,128)(2,1)S(1)} %bitcast.23,, ...), kind=kLoop, calls=%fused_computation.249 | loop fusion | flops 24316416 | bytes 16865280 | tf_op jit(solution)/shard_map/reduce_sum | solution.py:72
  164.7 12.4 %all-to-all-start.2 = ((f32[16,1,24,128]{3,2,1,0:T(8,128)}), f32[16,1,24,128]{3,2,1,0:T(8,128)S(1)}, u32[]{:S(2)}, u32[]{:S(2)}) async-start(f32[16,1,24,128]{3,2,1,0:T(8,128)} %bitcast.5), calls=%async_computation.2 | async-start | bytes 393216 | tf_op jit(solution)/shard_map/all_to_all | solution.py:37
  177.2 3.4 %collective-permute-start.5 = (bf16[2,3,48,768]{3,2,1,0:T(8,128)(2,1)S(1)}, bf16[2,3,48,768]{3,2,1,0:T(8,128)(2,1)S(1)}, u32[]{:S(2)}, u32[]{:S(2)}) collective-permute-start(bf16[2,3,48,768]{3,2,1,0:T(8,128)(2,1)S(1)} %get-tuple-element.121), channel_id=1, source_target_pairs={{0,1},{1,2},{2,3},{3,4},{4,5},{5,6},{6,7},{8,9},{9,10},{10,11},{11... | collective-permute-start | bytes 1327112 | tf_op jit(solution)/shard_map/ppermute | solution.py:25
  183.1 5.8 %all-to-all-done.2 = f32[16,1,24,128]{3,2,1,0:T(8,128)S(1)} async-done(((f32[16,1,24,128]{3,2,1,0:T(8,128)}), f32[16,1,24,128]{3,2,1,0:T(8,128)S(1)}, u32[]{:S(2)}, u32[]{:S(2)}) %all-to-all-start.2) | async-done | bytes 196640 | tf_op jit(solution)/shard_map/all_to_all | solution.py:37
  189.5 3.5 %all-to-all-start.3 = ((f32[16,1,24,128]{3,2,1,0:T(8,128)}), f32[16,1,24,128]{3,2,1,0:T(8,128)S(1)}, u32[]{:S(2)}, u32[]{:S(2)}) async-start(f32[16,1,24,128]{3,2,1,0:T(8,128)} %broadcast_in_dim.93), calls=%async_computation.3 | async-start | bytes 393216 | tf_op jit(solution)/shard_map/all_to_all | solution.py:43
  193.1 12.3 %all-to-all-done.3 = f32[16,1,24,128]{3,2,1,0:T(8,128)S(1)} async-done(((f32[16,1,24,128]{3,2,1,0:T(8,128)}), f32[16,1,24,128]{3,2,1,0:T(8,128)S(1)}, u32[]{:S(2)}, u32[]{:S(2)}) %all-to-all-start.3) | async-done | bytes 196640 | tf_op jit(solution)/shard_map/all_to_all | solution.py:43
  206.1 21.0 %all-to-all-start.4 = ((f32[16,1,24,128]{3,2,1,0:T(8,128)}), f32[16,1,24,128]{3,2,1,0:T(8,128)S(1)}, u32[]{:S(2)}, u32[]{:S(2)}) async-start(f32[16,1,24,128]{3,2,1,0:T(8,128)} %broadcast_in_dim.94), calls=%async_computation.4 | async-start | bytes 393216 | tf_op jit(solution)/shard_map/all_to_all | solution.py:43
  234.4 4.8 %all-to-all-start = ((bf16[8,12,1536]{2,1,0:T(8,128)(2,1)}), bf16[8,12,1536]{2,1,0:T(8,128)(2,1)S(1)}, u32[]{:S(2)}, u32[]{:S(2)}) async-start(bf16[8,12,1536]{2,1,0:T(8,128)(2,1)} %reshape.207), calls=%async_computation | async-start | bytes 786432 | tf_op jit(solution)/shard_map/all_to_all | solution.py:37
  239.2 15.9 %add_convert_fusion = bf16[2,6,48,768]{3,2,1,0:T(8,128)(2,1)} fusion(bf16[2,6,48,768]{3,2,1,0:T(8,128)(2,1)S(1)} %bitcast.26, bf16[2,3,48,768]{3,2,1,0:T(8,128)(2,1)} %collective-permute-done.6, bf16[2,3,48,768]{3,2,1,0:T(8,128)(2,1)} %copy-done.10, bf16[2,12,54,768]{3,2,1,0:T(8,128)(2,1)S(1)} %select_maximum_fusion, f32[768]{0:T(1024)} %copy-done.37, ...), kind=kLoop, calls=%fused_computation.259 | loop fusion | flops 68567040 | bytes 40848384 | tf_op jit(solution)/shard_map/convert_element_type | solution.py:134
  256.1 7.2 %all-to-all-start.1 = ((bf16[8,12,1536]{2,1,0:T(8,128)(2,1)}), bf16[8,12,1536]{2,1,0:T(8,128)(2,1)S(1)}, u32[]{:S(2)}, u32[]{:S(2)}) async-start(bf16[8,12,1536]{2,1,0:T(8,128)(2,1)} %broadcast_in_dim.80), calls=%async_computation.1 | async-start | bytes 786432 | tf_op jit(solution)/shard_map/all_to_all | solution.py:43
  264.6 7.9 %all-to-all-done.1 = bf16[8,12,1536]{2,1,0:T(8,128)(2,1)S(1)} async-done(((bf16[8,12,1536]{2,1,0:T(8,128)(2,1)}), bf16[8,12,1536]{2,1,0:T(8,128)(2,1)S(1)}, u32[]{:S(2)}, u32[]{:S(2)}) %all-to-all-start.1) | async-done | bytes 294944 | tf_op jit(solution)/shard_map/all_to_all | solution.py:43
  (240 shorter events, 50.4 us)
Async XLA Ops:
  7.2 83.8 %all-gather.2.cloned.1.call-start = ((), (), s32[]{:S(2)}) async-start(), calls=%async_computation.6 | async-start | bytes 5431296 | tf_op jit(solution)/shard_map/all_gather | solution.py:85
  9.7 15.2 %copy-start.4 = (bf16[2,6,48,768]{3,2,1,0:T(8,128)(2,1)S(1)}, bf16[2,6,48,768]{3,2,1,0:T(8,128)(2,1)}, u32[]{:S(2)}) copy-start(bf16[2,6,48,768]{3,2,1,0:T(8,128)(2,1)} %param.11) | copy-start | bytes 2654212
  9.7 220.2 %reduce-scatter.4.cloned.1.call-start = ((), (), s32[]{:S(2)}) async-start(), calls=%async_computation.7 | async-start | bytes 5013504 | tf_op jit(solution)/shard_map/reduce_scatter | solution.py:116
  11.1 13.8 %collective-permute-start = (bf16[2,3,48,768]{3,2,1,0:T(8,128)(2,1)S(1)}, bf16[2,3,48,768]{3,2,1,0:T(8,128)(2,1)S(1)}, u32[]{:S(2)}, u32[]{:S(2)}) collective-permute-start(bf16[2,3,48,768]{3,2,1,0:T(8,128)(2,1)S(1)} %get-tuple-element.125), channel_id=1, source_target_pairs={{0,1},{1,2},{2,3},{3,4},{4,5},{5,6},{6,7},{8,9},{9,10},{10,11},{11... | collective-permute-start | bytes 1327112 | tf_op jit(solution)/shard_map/ppermute | solution.py:25
  14.5 13.5 %collective-permute-start.1 = (bf16[2,3,48,768]{3,2,1,0:T(8,128)(2,1)S(1)}, bf16[2,3,48,768]{3,2,1,0:T(8,128)(2,1)S(1)}, u32[]{:S(2)}, u32[]{:S(2)}) collective-permute-start(bf16[2,3,48,768]{3,2,1,0:T(8,128)(2,1)S(1)} %get-tuple-element.126), channel_id=1, source_target_pairs={{1,0},{2,1},{3,2},{4,3},{5,4},{6,5},{7,6},{9,8},{10,9},{11,10},{12... | collective-permute-start | bytes 1327112 | tf_op jit(solution)/shard_map/ppermute | solution.py:26
  17.1 11.8 %copy-start.13 = (f32[768]{0:T(1024)}, f32[768]{0:T(1024)S(1)}, u32[]{:S(2)}) copy-start(f32[768]{0:T(1024)S(1)} %get-tuple-element.87) | copy-start | bytes 9220
  17.1 11.8 %copy-start.14 = (f32[768]{0:T(1024)}, f32[768]{0:T(1024)S(1)}, u32[]{:S(2)}) copy-start(f32[768]{0:T(1024)S(1)} %get-tuple-element.88) | copy-start | bytes 9220
  17.2 11.8 %copy-start.15 = (f32[768]{0:T(1024)}, f32[768]{0:T(1024)S(1)}, u32[]{:S(2)}) copy-start(f32[768]{0:T(1024)S(1)} %get-tuple-element.89) | copy-start | bytes 9220
  17.2 11.8 %copy-start.16 = (f32[768]{0:T(1024)}, f32[768]{0:T(1024)S(1)}, u32[]{:S(2)}) copy-start(f32[768]{0:T(1024)S(1)} %get-tuple-element.90) | copy-start | bytes 9220
  17.2 11.8 %copy-start.17 = (f32[768]{0:T(1024)}, f32[768]{0:T(1024)S(1)}, u32[]{:S(2)}) copy-start(f32[768]{0:T(1024)S(1)} %get-tuple-element.91) | copy-start | bytes 9220
  17.2 11.8 %copy-start.18 = (f32[768]{0:T(1024)}, f32[768]{0:T(1024)S(1)}, u32[]{:S(2)}) copy-start(f32[768]{0:T(1024)S(1)} %get-tuple-element.92) | copy-start | bytes 9220
  17.2 11.8 %copy-start.19 = (f32[768]{0:T(1024)}, f32[768]{0:T(1024)S(1)}, u32[]{:S(2)}) copy-start(f32[768]{0:T(1024)S(1)} %get-tuple-element.93) | copy-start | bytes 9220
  17.2 11.8 %copy-start.20 = (f32[768]{0:T(1024)}, f32[768]{0:T(1024)S(1)}, u32[]{:S(2)}) copy-start(f32[768]{0:T(1024)S(1)} %get-tuple-element.94) | copy-start | bytes 9220
  17.2 11.8 %copy-start.21 = (f32[768]{0:T(1024)}, f32[768]{0:T(1024)S(1)}, u32[]{:S(2)}) copy-start(f32[768]{0:T(1024)S(1)} %get-tuple-element.95) | copy-start | bytes 9220
  48.2 44.2 %collective-permute-start.3 = (bf16[576,768]{1,0:T(8,128)(2,1)}, bf16[576,768]{1,0:T(8,128)(2,1)}, u32[]{:S(2)}, u32[]{:S(2)}) collective-permute-start(bf16[576,768]{1,0:T(8,128)(2,1)} %get-tuple-element.115), channel_id=1, source_target_pairs={{0,8},{8,0},{1,9},{9,1},{2,10},{10,2},{3,11},{11,3},{4,12},{12,4},... | collective-permute-start | bytes 2654216 | tf_op jit(solution)/shard_map/ppermute | solution.py:31
  49.3 48.4 %collective-permute-start.2 = (bf16[576,768]{1,0:T(8,128)(2,1)}, bf16[576,768]{1,0:T(8,128)(2,1)}, u32[]{:S(2)}, u32[]{:S(2)}) collective-permute-start(bf16[576,768]{1,0:T(8,128)(2,1)} %fusion.138), channel_id=1, source_target_pairs={{0,8},{8,0},{1,9},{9,1},{2,10},{10,2},{3,11},{11,3},{4,12},{12,4},... | collective-permute-start | bytes 2654216 | tf_op jit(solution)/shard_map/ppermute | solution.py:31
  142.0 2.8 collective-permute-start.4
  164.7 24.1 %all-to-all-start.2 = ((f32[16,1,24,128]{3,2,1,0:T(8,128)}), f32[16,1,24,128]{3,2,1,0:T(8,128)S(1)}, u32[]{:S(2)}, u32[]{:S(2)}) async-start(f32[16,1,24,128]{3,2,1,0:T(8,128)} %bitcast.5), calls=%async_computation.2 | async-start | bytes 393216 | tf_op jit(solution)/shard_map/all_to_all | solution.py:37
  177.2 49.9 %collective-permute-start.5 = (bf16[2,3,48,768]{3,2,1,0:T(8,128)(2,1)S(1)}, bf16[2,3,48,768]{3,2,1,0:T(8,128)(2,1)S(1)}, u32[]{:S(2)}, u32[]{:S(2)}) collective-permute-start(bf16[2,3,48,768]{3,2,1,0:T(8,128)(2,1)S(1)} %get-tuple-element.121), channel_id=1, source_target_pairs={{0,1},{1,2},{2,3},{3,4},{4,5},{5,6},{6,7},{8,9},{9,10},{10,11},{11... | collective-permute-start | bytes 1327112 | tf_op jit(solution)/shard_map/ppermute | solution.py:25
  180.6 47.3 %collective-permute-start.6 = (bf16[2,3,48,768]{3,2,1,0:T(8,128)(2,1)S(1)}, bf16[2,3,48,768]{3,2,1,0:T(8,128)(2,1)}, u32[]{:S(2)}, u32[]{:S(2)}) collective-permute-start(bf16[2,3,48,768]{3,2,1,0:T(8,128)(2,1)S(1)} %get-tuple-element.122), channel_id=1, source_target_pairs={{1,0},{2,1},{3,2},{4,3},{5,4},{6,5},{7,6},{9,8},{10,9},{11,10},{12... | collective-permute-start | bytes 1327112 | tf_op jit(solution)/shard_map/ppermute | solution.py:26
  189.5 15.9 %all-to-all-start.3 = ((f32[16,1,24,128]{3,2,1,0:T(8,128)}), f32[16,1,24,128]{3,2,1,0:T(8,128)S(1)}, u32[]{:S(2)}, u32[]{:S(2)}) async-start(f32[16,1,24,128]{3,2,1,0:T(8,128)} %broadcast_in_dim.93), calls=%async_computation.3 | async-start | bytes 393216 | tf_op jit(solution)/shard_map/all_to_all | solution.py:43
  206.1 28.3 %all-to-all-start.4 = ((f32[16,1,24,128]{3,2,1,0:T(8,128)}), f32[16,1,24,128]{3,2,1,0:T(8,128)S(1)}, u32[]{:S(2)}, u32[]{:S(2)}) async-start(f32[16,1,24,128]{3,2,1,0:T(8,128)} %broadcast_in_dim.94), calls=%async_computation.4 | async-start | bytes 393216 | tf_op jit(solution)/shard_map/all_to_all | solution.py:43
  234.4 20.8 %all-to-all-start = ((bf16[8,12,1536]{2,1,0:T(8,128)(2,1)}), bf16[8,12,1536]{2,1,0:T(8,128)(2,1)S(1)}, u32[]{:S(2)}, u32[]{:S(2)}) async-start(bf16[8,12,1536]{2,1,0:T(8,128)(2,1)} %reshape.207), calls=%async_computation | async-start | bytes 786432 | tf_op jit(solution)/shard_map/all_to_all | solution.py:37
  256.1 16.4 %all-to-all-start.1 = ((bf16[8,12,1536]{2,1,0:T(8,128)(2,1)}), bf16[8,12,1536]{2,1,0:T(8,128)(2,1)S(1)}, u32[]{:S(2)}, u32[]{:S(2)}) async-start(bf16[8,12,1536]{2,1,0:T(8,128)(2,1)} %broadcast_in_dim.80), calls=%async_computation.1 | async-start | bytes 786432 | tf_op jit(solution)/shard_map/all_to_all | solution.py:43
  (48 other events, 389.9 us)
Sparse Core Ops, SparseCore 0:
  9.9 81.1 all-gather.1
  133.7 87.9 reduce-scatter.3
